TPU v7x, 32 devices: a whole 2x2x4 slice. The times are simulated.
32 devices in a mesh: mob: 2 (over x), imm: 16 (over z, y, core).
Axes of the slice: x: 2, y: 2, z: 4, core: 2. Of those that a mesh axis runs over, the one named last changes fastest.
Arguments:
- mobile_positions: float32 [512, 3, 128], P(('mob', 'imm')), may hold values from 0 to 4
- walk: float32 [2, 512, 3, 128], P(None, ('mob', 'imm')), may hold values from -1.8 to 1.8
- mobile_conc: float32 [512, 8, 128], P(('mob', 'imm')), may hold values from 0 to 2
- matrix_positions: float32 [512, 3, 128], P(('mob', 'imm')), may hold values from 0 to 4
- matrix_conc: float32 [512, 8, 128], P(('mob', 'imm')), may hold values from 0 to 2
- pair_rows: int32 [2, 16, 512], P('mob', 'imm'), may hold values from 0 to 255, as said below
- pair_cols: int32 [2, 16, 512], P('mob', 'imm'), may hold values from 0 to 31
- pair_counts: int32 [2, 16], P('mob', 'imm'), may hold values from 128 to 512, as said below
Outputs:
- mobile_after: float32 [512, 8, 128], P(('mob', 'imm'))
- matrix_after: float32 [512, 8, 128], P(('mob', 'imm'))
Inputs may be any that keep to these rules, and one draw needn't show every extreme that they name: Within one device the listed pairs (pair_rows, pair_cols) are distinct. `pair_counts`: in every draw some device uses all 512 slots.
All inputs are finite; a program needn't handle non-finite values.
Results may differ from a plain program's by a relative error of at most 0.0003.
Values sent between devices are 32-bit elements; how exact they have to be, the bound alone decides.
A program may use at most 64 MiB of HBM per device.

v0:
```python
import math

import jax
import jax.numpy as jnp
from jax import lax
from jax.sharding import PartitionSpec as P

RATE = 1.0 / 512.0


def pair_gains(mob_pos, imm_pos, mob_conc, imm_conc, valid):
    diff_x = mob_pos[:, 0, :, None] - imm_pos[:, 0, None, :]
    diff_y = mob_pos[:, 1, :, None] - imm_pos[:, 1, None, :]
    diff_z = mob_pos[:, 2, :, None] - imm_pos[:, 2, None, :]
    weight = (
        jnp.exp(-0.5 * (diff_x * diff_x + diff_y * diff_y + diff_z * diff_z)) * valid[:, None, None]
    )
    toward_m = jnp.einsum("kab,ksb->ksa", weight, imm_conc, precision=lax.Precision.HIGHEST)
    toward_i = jnp.einsum("kab,ksa->ksb", weight, mob_conc, precision=lax.Precision.HIGHEST)
    gain_m = RATE * (toward_m - jnp.sum(weight, axis=2)[:, None, :] * mob_conc)
    gain_i = RATE * (toward_i - jnp.sum(weight, axis=1)[:, None, :] * imm_conc)
    return (gain_m, gain_i)


def group_gains(positions, mob_conc, imm_pos, imm_conc, rows, cols, count):
    slots = rows.shape[0]
    block = math.gcd(64, slots)
    blocks_used = (count + block - 1) // block

    def one_block(step, accs):
        acc_m, acc_i = accs
        first = step * block
        rows_here = lax.dynamic_slice_in_dim(rows, first, block)
        cols_here = lax.dynamic_slice_in_dim(cols, first, block)
        slot_ids = first + jnp.arange(block, dtype=jnp.int32)
        valid = jnp.where(slot_ids < count, 1.0, 0.0).astype(jnp.float32)
        gain_m, gain_i = pair_gains(
            positions[rows_here],
            imm_pos[cols_here],
            mob_conc[rows_here],
            imm_conc[cols_here],
            valid,
        )
        return (acc_m.at[rows_here].add(gain_m), acc_i.at[cols_here].add(gain_i))

    start = (jnp.zeros_like(mob_conc), jnp.zeros_like(imm_conc))
    return lax.fori_loop(0, blocks_used, one_block, start)


def on_device(
    mobile_positions,
    walk,
    mobile_conc,
    matrix_positions,
    matrix_conc,
    pair_rows,
    pair_cols,
    pair_counts,
):
    moved_one = mobile_positions + walk[0]
    moved_two = moved_one + walk[1]
    moved = jnp.stack([moved_one, moved_two], axis=1)
    group_moved, group_mconc = (
        lax.all_gather(moved, "imm", axis=0, tiled=True),
        lax.all_gather(mobile_conc, "imm", axis=0, tiled=True),
    )
    group_ipos, group_iconc = (
        lax.all_gather(matrix_positions, "mob", axis=0, tiled=True),
        lax.all_gather(matrix_conc, "mob", axis=0, tiled=True),
    )
    rows = pair_rows[0, 0]
    cols = pair_cols[0, 0]
    count = pair_counts[0, 0]
    mob_part, imm_part = group_gains(
        group_moved[:, 0], group_mconc, group_ipos, group_iconc, rows, cols, count
    )
    own_mob = mobile_conc + lax.psum_scatter(mob_part, "imm", scatter_dimension=0, tiled=True)
    own_imm = matrix_conc + lax.psum_scatter(imm_part, "mob", scatter_dimension=0, tiled=True)
    next_mconc = lax.all_gather(own_mob, "imm", axis=0, tiled=True)
    next_iconc = lax.all_gather(own_imm, "mob", axis=0, tiled=True)
    mob_part, imm_part = group_gains(
        group_moved[:, 1], next_mconc, group_ipos, next_iconc, rows, cols, count
    )
    mobile_after = own_mob + lax.psum_scatter(mob_part, "imm", scatter_dimension=0, tiled=True)
    matrix_after = own_imm + lax.psum_scatter(imm_part, "mob", scatter_dimension=0, tiled=True)
    return (mobile_after, matrix_after)


def solution(mesh):
    return jax.shard_map(
        on_device,
        mesh=mesh,
        in_specs=(
            P(("mob", "imm"), None, None),
            P(None, ("mob", "imm"), None, None),
            P(("mob", "imm"), None, None),
            P(("mob", "imm"), None, None),
            P(("mob", "imm"), None, None),
            P("mob", "imm", None),
            P("mob", "imm", None),
            P("mob", "imm"),
        ),
        out_specs=(P(("mob", "imm"), None, None), P(("mob", "imm"), None, None)),
        check_vma=False,
    )
```

profile of v0, /device:TPU:0, one launch (start us, length us, event | category | flops | bytes accessed | tf_op | source)
XLA Modules:
  0.0 777.9 jit_solution(1335252484954916221)
XLA Ops:
  8.6 5.7 all_gather.20
  14.3 5.2 all_gather.18
  21.1 26.7 %all_gather.19 = f32[256,2,3,128]{3,2,0,1:T(4,128)S(1)} all-gather(f32[16,2,3,128]{3,2,0,1:T(4,128)S(1)} %pad_maximum_fusion), channel_id=1, replica_groups=mesh['mob'=2,'imm'=16] {'imm'}, dimensions={0}, use_global_device_ids=true | all-gather | bytes 835584 | tf_op jit(solution)/shard_map/all_gather | solution.py:64
  47.9 4.5 all-gather.3.cloned.1.call-done
  52.5 100.8 %while.24 = (s32[]{:T(128)}, f32[256,8,128]{2,1,0:T(8,128)S(1)}, f32[32,8,128]{2,1,0:T(8,128)S(1)}, s32[]{:T(128)}, s32[512]{0:T(512)S(1)}, /*index=5*/s32[512]{...) while((s32[]{:T(128)}, f32[256,8,128]{2,1,0:T(8,128)S(1)}, ...), condition=%wide.region_5.6_spmd, body=%wide.region_0.5_spmd.sunk | while | flops 235391552 | bytes 5714119 | solution.py:47
  54.8 5.3 fusion.83
  62.6 7.7 fusion.85
  73.1 10.3 %fusion.84 = f32[64,8,128]{2,1,0:T(8,128)S(1)} fusion(f32[64,8,128]{2,1,0:T(8,128)S(1)} %gather_fusion, f32[64]{0:T(128)S(1)} %compare_select_fusion.11, f32[64,128]{1,0:T(8,128)S(1)} %bitcast.82, f32[64,128]{1,0:T(8,128)S(1)} %bitcast.100, f32[64,128]{1,0:T(8,128)S(1)} %bitcast.79, f32[64,128]{1,0:T(8,128)S(1)} %bitcast.97, ...), kind=kOutput, calls=%fused_computation.34.clone.1 | convolution fusion | flops 111345664 | bytes 1016064 | tf_op jit(solution)/shard_map/while/body/kab,ksb->ksa/dot_general | solution.py:18
  88.4 5.3 fusion.83
  96.2 7.7 fusion.85
  103.9 2.8 scatter_fusion.1
  106.7 10.3 %fusion.84 = f32[64,8,128]{2,1,0:T(8,128)S(1)} fusion(f32[64,8,128]{2,1,0:T(8,128)S(1)} %gather_fusion, f32[64]{0:T(128)S(1)} %compare_select_fusion.11, f32[64,128]{1,0:T(8,128)S(1)} %bitcast.82, f32[64,128]{1,0:T(8,128)S(1)} %bitcast.100, f32[64,128]{1,0:T(8,128)S(1)} %bitcast.79, f32[64,128]{1,0:T(8,128)S(1)} %bitcast.97, ...), kind=kOutput, calls=%fused_computation.34.clone.1 | convolution fusion | flops 111345664 | bytes 1016064 | tf_op jit(solution)/shard_map/while/body/kab,ksb->ksa/dot_general | solution.py:18
  122.0 5.3 fusion.83
  129.8 7.7 fusion.85
  140.3 10.3 %fusion.84 = f32[64,8,128]{2,1,0:T(8,128)S(1)} fusion(f32[64,8,128]{2,1,0:T(8,128)S(1)} %gather_fusion, f32[64]{0:T(128)S(1)} %compare_select_fusion.11, f32[64,128]{1,0:T(8,128)S(1)} %bitcast.82, f32[64,128]{1,0:T(8,128)S(1)} %bitcast.100, f32[64,128]{1,0:T(8,128)S(1)} %bitcast.79, f32[64,128]{1,0:T(8,128)S(1)} %bitcast.97, ...), kind=kOutput, calls=%fused_computation.34.clone.1 | convolution fusion | flops 111345664 | bytes 1016064 | tf_op jit(solution)/shard_map/while/body/kab,ksb->ksa/dot_general | solution.py:18
  155.1 222.7 %reduce-scatter.5.cloned.1.call-done = f32[16,8,128]{2,1,0:T(8,128)} async-done(((f32[256,8,128]{2,1,0:T(8,128)}), f32[16,8,128]{2,1,0:T(8,128)}) %reduce-scatter.5.cloned.1.call-update) | async-done | bytes 65552 | tf_op jit(solution)/shard_map/reduce_scatter | solution.py:77
  379.4 10.0 %reduce-scatter.7.cloned.1.call-done = f32[16,8,128]{2,1,0:T(8,128)} async-done(((f32[32,8,128]{2,1,0:T(8,128)}), f32[16,8,128]{2,1,0:T(8,128)}) %reduce-scatter.7.cloned.1.call-update) | async-done | bytes 65552 | tf_op jit(solution)/shard_map/reduce_scatter | solution.py:78
  390.2 4.9 all_gather.22
  395.2 35.0 %all-gather.5.cloned.1.call-done = f32[256,8,128]{2,1,0:T(8,128)} async-done(((f32[16,8,128]{2,1,0:T(8,128)}), f32[256,8,128]{2,1,0:T(8,128)}) %all-gather.5.cloned.1.call-update) | async-done | bytes 1048592 | tf_op jit(solution)/shard_map/all_gather | solution.py:79
  430.3 100.8 %while.25 = (s32[]{:T(128)}, f32[256,8,128]{2,1,0:T(8,128)S(1)}, f32[32,8,128]{2,1,0:T(8,128)S(1)}, s32[]{:T(128)}, s32[512]{0:T(512)S(1)}, /*index=5*/s32[512]{...) while((s32[]{:T(128)}, f32[256,8,128]{2,1,0:T(8,128)S(1)}, ...), condition=%wide.region_13.14_spmd, body=%wide.region_8.13_spmd.sunk | while | flops 235391552 | bytes 5714119 | solution.py:47
  432.6 5.3 fusion.90
  440.3 7.7 fusion.92
  450.8 10.3 %fusion.91 = f32[64,8,128]{2,1,0:T(8,128)S(1)} fusion(f32[64,8,128]{2,1,0:T(8,128)S(1)} %gather_fusion.4, f32[64]{0:T(128)S(1)} %compare_select_fusion.13, f32[64,128]{1,0:T(8,128)S(1)} %bitcast.91, f32[64,128]{1,0:T(8,128)S(1)} %bitcast.109, f32[64,128]{1,0:T(8,128)S(1)} %bitcast.88, f32[64,128]{1,0:T(8,128)S(1)} %bitcast.106, ...), kind=kOutput, calls=%fused_computation.66.clone.1 | convolution fusion | flops 111345664 | bytes 1016064 | tf_op jit(solution)/shard_map/while/body/kab,ksb->ksa/dot_general | solution.py:18
  466.2 5.3 fusion.90
  473.9 7.7 fusion.92
  481.7 2.8 scatter_fusion.3
  484.4 10.3 %fusion.91 = f32[64,8,128]{2,1,0:T(8,128)S(1)} fusion(f32[64,8,128]{2,1,0:T(8,128)S(1)} %gather_fusion.4, f32[64]{0:T(128)S(1)} %compare_select_fusion.13, f32[64,128]{1,0:T(8,128)S(1)} %bitcast.91, f32[64,128]{1,0:T(8,128)S(1)} %bitcast.109, f32[64,128]{1,0:T(8,128)S(1)} %bitcast.88, f32[64,128]{1,0:T(8,128)S(1)} %bitcast.106, ...), kind=kOutput, calls=%fused_computation.66.clone.1 | convolution fusion | flops 111345664 | bytes 1016064 | tf_op jit(solution)/shard_map/while/body/kab,ksb->ksa/dot_general | solution.py:18
  499.8 5.3 fusion.90
  507.5 7.7 fusion.92
  518.0 10.3 %fusion.91 = f32[64,8,128]{2,1,0:T(8,128)S(1)} fusion(f32[64,8,128]{2,1,0:T(8,128)S(1)} %gather_fusion.4, f32[64]{0:T(128)S(1)} %compare_select_fusion.13, f32[64,128]{1,0:T(8,128)S(1)} %bitcast.91, f32[64,128]{1,0:T(8,128)S(1)} %bitcast.109, f32[64,128]{1,0:T(8,128)S(1)} %bitcast.88, f32[64,128]{1,0:T(8,128)S(1)} %bitcast.106, ...), kind=kOutput, calls=%fused_computation.66.clone.1 | convolution fusion | flops 111345664 | bytes 1016064 | tf_op jit(solution)/shard_map/while/body/kab,ksb->ksa/dot_general | solution.py:18
  532.4 175.8 %reduce-scatter.11.cloned.1.call-done = f32[16,8,128]{2,1,0:T(8,128)} async-done(((f32[32,8,128]{2,1,0:T(8,128)}), f32[16,8,128]{2,1,0:T(8,128)}) %reduce-scatter.11.cloned.1.call-update) | async-done | bytes 65552 | tf_op jit(solution)/shard_map/reduce_scatter | solution.py:85
  709.6 59.9 %reduce-scatter.9.cloned.1.call-done = f32[16,8,128]{2,1,0:T(8,128)} async-done(((f32[256,8,128]{2,1,0:T(8,128)}), f32[16,8,128]{2,1,0:T(8,128)}) %reduce-scatter.9.cloned.1.call-update) | async-done | bytes 65552 | tf_op jit(solution)/shard_map/reduce_scatter | solution.py:84
  (113 shorter events, 66.3 us)
Async XLA Ops:
  7.2 45.3 %all-gather.3.cloned.1.call-start = ((), (), s32[]{:S(2)}) async-start(), calls=%async_computation.4 | async-start | bytes 1114112 | tf_op jit(solution)/shard_map/all_gather | solution.py:65
  7.9 369.9 %reduce-scatter.5.cloned.1.call-start = ((), (), s32[]{:S(2)}) async-start(), calls=%async_computation.5 | async-start | bytes 1114112 | tf_op jit(solution)/shard_map/reduce_scatter | solution.py:77
  47.9 4.6 copy-start.7
  47.9 4.6 copy-start.8
  153.4 1.0 copy-start.3
  153.4 1.0 copy-start.1
  153.4 224.5 %copy-start.6 = (f32[16,8,128]{2,1,0:T(8,128)S(1)}, f32[16,8,128]{2,1,0:T(8,128)}, u32[]{:S(2)}) copy-start(f32[16,8,128]{2,1,0:T(8,128)} %param.14) | copy-start | bytes 196612
  153.4 236.0 %copy-start.5 = (f32[16,8,128]{2,1,0:T(8,128)S(1)}, f32[16,8,128]{2,1,0:T(8,128)}, u32[]{:S(2)}) copy-start(f32[16,8,128]{2,1,0:T(8,128)} %param.16) | copy-start | bytes 196612
  154.4 235.0 %reduce-scatter.7.cloned.1.call-start = ((), (), s32[]{:S(2)}) async-start(), calls=%async_computation.6 | async-start | bytes 196608 | tf_op jit(solution)/shard_map/reduce_scatter | solution.py:78
  155.1 275.1 %all-gather.5.cloned.1.call-start = ((), (), s32[]{:S(2)}) async-start(), calls=%async_computation.7 | async-start | bytes 1114112 | tf_op jit(solution)/shard_map/all_gather | solution.py:79
  379.3 328.8 %reduce-scatter.11.cloned.1.call-start = ((), (), s32[]{:S(2)}) async-start(), calls=%async_computation.9 | async-start | bytes 196608 | tf_op jit(solution)/shard_map/reduce_scatter | solution.py:85
  531.1 0.6 copy-start
  531.1 1.0 copy-start.2
  531.1 238.4 %copy-start.4 = (f32[16,8,128]{2,1,0:T(8,128)S(1)}, f32[16,8,128]{2,1,0:T(8,128)}, u32[]{:S(2)}) copy-start(f32[16,8,128]{2,1,0:T(8,128)} %add.108) | copy-start | bytes 196612
  531.8 237.8 %reduce-scatter.9.cloned.1.call-start = ((), (), s32[]{:S(2)}) async-start(), calls=%async_computation.8 | async-start | bytes 1114112 | tf_op jit(solution)/shard_map/reduce_scatter | solution.py:84
Sparse Core Ops, SparseCore 0:
  10.2 42.2 all-gather.2
  154.5 223.3 reduce-scatter.4
  380.1 9.2 reduce-scatter.6
  392.2 37.9 all-gather.4
  531.9 176.2 reduce-scatter.10
  712.1 57.4 reduce-scatter.8
where the time goes:
time: 779 us; the launch traced here: 778 us
  waiting for transfers between devices  510 us (65%)
  matrix products  108 us (14%)
  other arithmetic  75.3 us (10%)
  blocking collectives  42.4 us (5%)
  local copies, waits for them, and re-layouts  26.4 us (3%)
  between operations  14.9 us (2%)
    reduce_scatter x2, waiting for transfers between devices, on_device(): lax.psum_scatter(mob_part, 'imm', scatter_dimension=0, tiled=True)  283 us
    reduce_scatter x2, waiting for transfers between devices, on_device(): lax.psum_scatter(imm_part, 'mob', scatter_dimension=0, tiled=True)  186 us
    dot_general x6, matrix products, pair_gains(): jnp.einsum('kab,ksb->ksa', weight, imm_conc, precision=lax.Precision.HIGH...  61.9 us
    dot_general x6, matrix products, pair_gains(): jnp.einsum('kab,ksa->ksb', weight, mob_conc, precision=lax.Precision.HIGH...  46.4 us
    all_gather x1, waiting for transfers between devices, on_device(): next_mconc = lax.all_gather(own_mob, 'imm', axis=0, tiled=True)  35 us
    scatter-add x12, other arithmetic, one_block(): return (acc_m.at[rows_here].add(gain_m), acc_i.at[cols_here].add(gain_i))  33 us
    reduce_sum x6, other arithmetic, pair_gains(): gain_i = RATE * (toward_i - jnp.sum(weight, axis=1)[:, None, :] * imm_conc)  31.8 us
    all_gather x1, blocking collectives, on_device(): lax.all_gather(moved, 'imm', axis=0, tiled=True)  26.7 us
  transfers between devices with their start and end apart: 6, of which 6 were waited for; matrix products, arithmetic and copies ran while one was open for 1% of the time, Pallas kernels for 0%

commit v1 on v0

v1 whole, which is shorter than its diff:
```python
import functools
import math

import jax
import jax.numpy as jnp
from jax import lax
from jax.experimental import pallas as pl
from jax.experimental.pallas import tpu as pltpu
from jax.sharding import PartitionSpec as P

RATE = 1.0 / 512.0
SCALE = math.sqrt(0.5 * math.log2(math.e))
CENTRE = 2.0
MESH = pl.DeviceIdType.MESH
VMEM_LIMIT = 48 * 1024 * 1024
UNROLL = 4
GROUPS = 6


class Place:
    def __init__(self, n_mob, n_imm):
        rest = n_imm // 2
        nb = 1
        while nb * nb * 4 <= rest:
            nb *= 2
        self.nm, self.nb, self.na = n_mob, nb, rest // nb
        self.p = lax.axis_index("mob")
        q = lax.axis_index("imm")
        self.core = lax.rem(q, 2)
        chip = lax.div(q, 2)
        self.b = lax.rem(chip, nb)
        self.a = lax.div(chip, nb)

    def am(self, d):
        return lax.rem(self.a + (d + self.na), self.na)

    def bm(self, d):
        return lax.rem(self.b + (d + self.nb), self.nb)

    def pm(self, d):
        return lax.rem(self.p + (d + self.nm), self.nm)

    def dev(self, a, b, core):
        return (self.p, (a * self.nb + b) * 2 + core)

    def sibling(self):
        return self.dev(self.a, self.b, 1 - self.core)

    def across(self, d):
        return (self.pm(d), (self.a * self.nb + self.b) * 2 + self.core)

    def barrier(self):
        sem = pltpu.get_barrier_semaphore()
        peers = [self.sibling()]
        peers += [self.dev(self.a, self.bm(d), self.core) for d in range(1, self.nb)]
        peers += [self.dev(self.am(d), self.b, self.core) for d in range(1, self.na)]
        peers += [self.across(d) for d in range(1, self.nm)]
        for peer in peers:
            pl.semaphore_signal(sem, inc=1, device_id=peer, device_id_type=MESH)
        pl.semaphore_wait(sem, len(peers))


def remote(src, dst, send, recv, device):
    copy = pltpu.make_async_remote_copy(
        src_ref=src, dst_ref=dst, send_sem=send, recv_sem=recv, device_id=device, device_id_type=MESH
    )
    copy.start()
    return copy


def gather_imm(at, refs, sems):
    a_send, a_recv, b_send, b_recv, c_send, c_recv = sems
    na, nb = at.na, at.nb
    sends, a_copies, b_copies, c_copies = [], {}, {}, {}
    for da in range(1, na):
        for i, g in enumerate(refs):
            block = g.at[at.a, at.b, at.core]
            a_copies[da, i] = remote(
                block, block, a_send.at[i, da], a_recv.at[i, da], at.dev(at.am(da), at.b, at.core)
            )
    for da in range(na):
        for i, g in enumerate(refs):
            if da:
                a_copies[da, i].wait_recv()
            block = g.at[at.am(-da), at.b, at.core]
            for db in range(1, nb):
                b_copies[da, db, i] = remote(
                    block, block, b_send.at[i, da, db], b_recv.at[i, da, db], at.dev(at.a, at.bm(db), at.core)
                )
            c_copies[da, 0, i] = remote(
                block, block, c_send.at[i, da, 0], c_recv.at[i, da, 0], at.sibling()
            )
    for da in range(na):
        for db in range(1, nb):
            for i, g in enumerate(refs):
                b_copies[da, db, i].wait_recv()
                block = g.at[at.am(-da), at.bm(-db), at.core]
                c_copies[da, db, i] = remote(
                    block, block, c_send.at[i, da, db], c_recv.at[i, da, db], at.sibling()
                )
    for copy in c_copies.values():
        copy.wait_recv()
    for copies in (a_copies, b_copies, c_copies):
        for copy in copies.values():
            copy.wait_send()


def gather_mob_start(at, refs, send, recv):
    copies = []
    for dp in range(1, at.nm):
        for i, g in enumerate(refs):
            block = g.at[at.p]
            copies.append(remote(block, block, send.at[i, dp], recv.at[i, dp], at.across(dp)))
    return copies


def reduce_mob_start(at, part, land, send, recv):
    return [
        remote(part.at[at.pm(dp)], land.at[dp], send.at[dp], recv.at[dp], at.across(dp))
        for dp in range(1, at.nm)
    ]


def reduce_imm(at, part, land_c, land_b, land_a, out_b, out_a, sems):
    a_send, a_recv, b_send, b_recv, c_send, c_recv = sems
    na, nb = at.na, at.nb
    order = list(range(1, na)) + [0]
    a_copies, b_copies, c_copies = {}, {}, {}
    for db in list(range(1, nb)) + [0]:
        for da in order:
            c_copies[da, db] = remote(
                part.at[at.am(da), at.bm(db), 1 - at.core],
                land_c.at[da, db],
                c_send.at[da, db],
                c_recv.at[da, db],
                at.sibling(),
            )
    for da in order:
        for db in range(1, nb):
            c_copies[da, db].wait_recv()
            out_b[da, db] = part[at.am(da), at.bm(db), at.core] + land_c[da, db]
            b_copies[da, db] = remote(
                out_b.at[da, db],
                land_b.at[da, db],
                b_send.at[da, db],
                b_recv.at[da, db],
                at.dev(at.a, at.bm(db), at.core),
            )
    total = None
    for da in order:
        c_copies[da, 0].wait_recv()
        here = part[at.am(da), at.b, at.core] + land_c[da, 0]
        for db in range(1, nb):
            b_copies[da, db].wait_recv()
            here = here + land_b[da, db]
        if da:
            out_a[da] = here
            a_copies[da] = remote(
                out_a.at[da], land_a.at[da], a_send.at[da], a_recv.at[da], at.dev(at.am(da), at.b, at.core)
            )
        else:
            total = here
    for da in range(1, na):
        a_copies[da].wait_recv()
        total = total + land_a[da]
    for copies in (a_copies, b_copies, c_copies):
        for copy in copies.values():
            copy.wait_send()
    return total


def first_gather(n_mob, n_imm, mpos, walk, mconc, ipos, iconc, g_pos, g_conc, h_pos, h_conc, *sems):
    at = Place(n_mob, n_imm)
    own = g_pos.at[at.a, at.b, at.core]
    moved = mpos[...]
    for step in range(2):
        moved = moved + walk[step]
        x = (moved - CENTRE) * SCALE
        own[:, 4 * step : 4 * step + 3, :] = x
        own[:, 4 * step + 3 : 4 * step + 4, :] = -jnp.sum(x * x, axis=1, keepdims=True)
    g_conc[at.a, at.b, at.core] = mconc[...]
    h_own = h_pos.at[at.p]
    y = (ipos[...] - CENTRE) * SCALE
    h_own[:, 0:3, :] = 2.0 * y
    h_own[:, 3:4, :] = jnp.ones_like(y[:, 0:1, :])
    h_own[:, 4:5, :] = -jnp.sum(y * y, axis=1, keepdims=True)
    h_own[:, 5:8, :] = jnp.zeros_like(y)
    h_conc[at.p] = iconc[...]
    at.barrier()
    mob = gather_mob_start(at, (h_pos, h_conc), *sems[6:])
    gather_imm(at, (g_conc, g_pos), sems[:6])
    for copy in mob:
        copy.wait()


def exchange(n_mob, n_imm, part_m, part_i, conc_m, conc_i, own_m, own_i, g_conc, h_conc,
             land_c, land_b, land_a, out_b, out_a, land_m, *sems):
    at = Place(n_mob, n_imm)
    at.barrier()
    mob = reduce_mob_start(at, part_i, land_m, *sems[6:8])
    total = conc_m[...] + reduce_imm(at, part_m, land_c, land_b, land_a, out_b, out_a, sems[:6])
    own_m[...] = total
    g_conc[at.a, at.b, at.core] = total
    total = conc_i[...] + part_i[at.p]
    for dp, copy in enumerate(mob, 1):
        copy.wait()
        total = total + land_m[dp]
    own_i[...] = total
    h_conc[at.p] = total
    mob = gather_mob_start(at, (h_conc,), *sems[8:10])
    gather_imm(at, (g_conc,), sems[10:16])
    for copy in mob:
        copy.wait()


def last_reduce(n_mob, n_imm, part_m, part_i, conc_m, conc_i, own_m, own_i,
                land_c, land_b, land_a, out_b, out_a, land_m, *sems):
    at = Place(n_mob, n_imm)
    at.barrier()
    mob = reduce_mob_start(at, part_i, land_m, *sems[6:8])
    own_m[...] = conc_m[...] + reduce_imm(at, part_m, land_c, land_b, land_a, out_b, out_a, sems[:6])
    total = conc_i[...] + part_i[at.p]
    for dp, copy in enumerate(mob, 1):
        copy.wait()
        total = total + land_m[dp]
    own_i[...] = total


def split3(x):
    high = x.astype(jnp.bfloat16).astype(jnp.float32)
    rest = x - high
    mid = rest.astype(jnp.bfloat16).astype(jnp.float32)
    return high, mid, rest - mid


def conc_rows(conc):
    high = conc.astype(jnp.bfloat16).astype(jnp.float32)
    ones = jnp.ones_like(conc)
    return jnp.concatenate([high, conc - high, ones, ones], axis=0).astype(jnp.bfloat16)


def pair_loop(step, rows, cols, count, x_pos, x_conc, y_pos, y_conc, gain_m, gain_i, y_split):
    gain_m[...] = jnp.zeros_like(gain_m)
    gain_i[...] = jnp.zeros_like(gain_i)

    def prepare(c, carry):
        h, m, l = split3(y_pos[c])
        zeros = jnp.zeros((128 - 8 * GROUPS, 128), jnp.float32)
        stacked = jnp.concatenate([h, h, h, m, m, l, zeros], axis=0)
        y_split[c] = stacked.T.astype(jnp.bfloat16)
        return carry

    lax.fori_loop(0, y_pos.shape[0], prepare, 0)
    row = lax.broadcasted_iota(jnp.int32, (8, 128), 0)
    keep = row < 4
    unit = jnp.where(row == 4, 1.0, 0.0).astype(jnp.float32)
    zeros = jnp.zeros((128 - 8 * GROUPS, 128), jnp.float32)
    used = count[0, 0]

    def body(block, carry):
        results = []
        for u in range(UNROLL):
            k = block * UNROLL + u
            r, c = rows[0, 0, k], cols[0, 0, k]
            x = x_pos[r]
            if step:
                x = pltpu.roll(x, 4, 0)
            h, m, l = split3(jnp.where(keep, x, unit))
            x_split = jnp.concatenate([h, m, l, h, m, h, zeros], axis=0).astype(jnp.bfloat16)
            power = jnp.dot(y_split[c], x_split, preferred_element_type=jnp.float32)
            weight = jnp.exp2(power).astype(jnp.bfloat16)
            cm, ci = x_conc[r], y_conc[c]
            to_m = jnp.dot(conc_rows(ci), weight, preferred_element_type=jnp.float32)
            to_i = lax.dot_general(
                conc_rows(cm), weight, (((1,), (1,)), ((), ())), preferred_element_type=jnp.float32
            )
            rate = jnp.where(k < used, RATE, 0.0).astype(jnp.float32)
            add_m = rate * (to_m[0:8] + to_m[8:16] - to_m[16:24] * cm)
            add_i = rate * (to_i[0:8] + to_i[8:16] - to_i[16:24] * ci)
            results.append((r, c, add_m, add_i))
        for r, c, add_m, add_i in results:
            gain_m[r] += add_m
            gain_i[c] += add_i
        return carry

    lax.fori_loop(0, lax.div(used + (UNROLL - 1), UNROLL), body, 0)


def on_device(n_mob, n_imm, mpos, walk, mconc, ipos, iconc, rows, cols, counts):
    rest = n_imm // 2
    nb = 1
    while nb * nb * 4 <= rest:
        nb *= 2
    na = rest // nb
    f32 = jnp.float32
    mc, solutes, part = mconc.shape
    ic = iconc.shape[0]
    vmem = pl.BlockSpec(memory_space=pltpu.VMEM)
    smem = pl.BlockSpec(memory_space=pltpu.SMEM)
    dma = pltpu.SemaphoreType.DMA

    def params(ident):
        return pltpu.CompilerParams(collective_id=ident, has_side_effects=True, vmem_limit_bytes=VMEM_LIMIT)

    def gather_sems(refs):
        return [dma((refs, na))] * 2 + [dma((refs, na, nb))] * 4

    reduce_sems = [dma((na,))] * 2 + [dma((na, nb))] * 4
    cell_m = (mc, solutes, part)
    cell_i = (ic, solutes, part)
    all_m = jax.ShapeDtypeStruct((na, nb, 2) + cell_m, f32)
    all_i = jax.ShapeDtypeStruct((n_mob,) + cell_i, f32)
    g_pos, g_conc, h_pos, h_conc = pl.pallas_call(
        functools.partial(first_gather, n_mob, n_imm),
        out_shape=(all_m, all_m, all_i, all_i),
        in_specs=[vmem] * 5,
        out_specs=(vmem,) * 4,
        scratch_shapes=gather_sems(2) + [dma((2, n_mob))] * 2,
        compiler_params=params(0),
    )(mpos, walk, mconc, ipos, iconc)

    flat_m = (n_imm * mc, solutes, part)
    flat_i = (n_mob * ic, solutes, part)

    def pairs(step, x_conc, y_conc):
        gains = pl.pallas_call(
            functools.partial(pair_loop, step),
            out_shape=(jax.ShapeDtypeStruct(flat_m, f32), jax.ShapeDtypeStruct(flat_i, f32)),
            in_specs=[smem] * 3 + [vmem] * 4,
            out_specs=(vmem,) * 2,
            scratch_shapes=[pltpu.VMEM((flat_i[0], part, 128), jnp.bfloat16)],
            compiler_params=pltpu.CompilerParams(vmem_limit_bytes=VMEM_LIMIT),
        )(
            rows,
            cols,
            counts,
            g_pos.reshape(flat_m),
            x_conc.reshape(flat_m),
            h_pos.reshape(flat_i),
            y_conc.reshape(flat_i),
        )
        return gains[0].reshape(all_m.shape), gains[1].reshape(all_i.shape)

    lands = [
        pltpu.VMEM((na, nb) + cell_m, f32),
        pltpu.VMEM((na, nb) + cell_m, f32),
        pltpu.VMEM((na,) + cell_m, f32),
        pltpu.VMEM((na, nb) + cell_m, f32),
        pltpu.VMEM((na,) + cell_m, f32),
        pltpu.VMEM((n_mob,) + cell_i, f32),
    ]
    own = (jax.ShapeDtypeStruct(cell_m, f32), jax.ShapeDtypeStruct(cell_i, f32))
    part_m, part_i = pairs(0, g_conc, h_conc)
    own_m, own_i, g_conc, h_conc = pl.pallas_call(
        functools.partial(exchange, n_mob, n_imm),
        out_shape=own + (all_m, all_i),
        in_specs=[vmem] * 4,
        out_specs=(vmem,) * 4,
        scratch_shapes=lands + reduce_sems + [dma((n_mob,))] * 2 + [dma((1, n_mob))] * 2 + gather_sems(1),
        compiler_params=params(1),
    )(part_m, part_i, mconc, iconc)
    part_m, part_i = pairs(1, g_conc, h_conc)
    return pl.pallas_call(
        functools.partial(last_reduce, n_mob, n_imm),
        out_shape=own,
        in_specs=[vmem] * 4,
        out_specs=(vmem,) * 2,
        scratch_shapes=lands + reduce_sems + [dma((n_mob,))] * 2,
        compiler_params=params(2),
    )(part_m, part_i, own_m, own_i)


def solution(mesh):
    return jax.shard_map(
        functools.partial(on_device, mesh.shape["mob"], mesh.shape["imm"]),
        mesh=mesh,
        in_specs=(
            P(("mob", "imm"), None, None),
            P(None, ("mob", "imm"), None, None),
            P(("mob", "imm"), None, None),
            P(("mob", "imm"), None, None),
            P(("mob", "imm"), None, None),
            P("mob", "imm", None),
            P("mob", "imm", None),
            P("mob", "imm"),
        ),
        out_specs=(P(("mob", "imm"), None, None), P(("mob", "imm"), None, None)),
        check_vma=False,
    )
```

time: 779 us -> 235 us (0.30)
  waiting for transfers between devices: 510 us -> 0 us
  Pallas kernels: 0 us -> 230 us
  matrix products: 108 us -> 0 us
  other arithmetic: 75.3 us -> 0 us
  blocking collectives: 42.4 us -> 0 us
  local copies, waits for them, and re-layouts: 26.4 us -> 3.57 us
  between operations: 14.9 us -> 1.41 us
    reduce_scatter x4 -> x0, waiting for transfers between devices: 468 us -> none  [the longest x2 283 us: on_device(): lax.psum_scatter(mob_part, 'imm', scatter_dimension=0, tiled=True)]
    pallas_call x0 -> x5, Pallas kernels: none -> 230 us  [the longest x1 83.3 us: on_device(): pl.pallas_call(functools.partial(exchange, n_mob, n_imm), out_shape=own +...]
    dot_general x12 -> x0, matrix products: 108 us -> none  [the longest x6 61.9 us: pair_gains(): jnp.einsum('kab,ksb->ksa', weight, imm_conc, precision=lax.Precision.HIGH...]
    all_gather x4 -> x0, blocking collectives: 42.4 us -> none  [the longest x1 26.7 us: on_device(): lax.all_gather(moved, 'imm', axis=0, tiled=True)]
    all_gather x2 -> x0, waiting for transfers between devices: 39.5 us -> none  [the longest x1 35 us: on_device(): next_mconc = lax.all_gather(own_mob, 'imm', axis=0, tiled=True)]
    scatter-add x12 -> x0, other arithmetic: 33 us -> none  [one_block(): return (acc_m.at[rows_here].add(gain_m), acc_i.at[cols_here].add(gain_i))]
    reduce_sum x6 -> x0, other arithmetic: 31.8 us -> none  [pair_gains(): gain_i = RATE * (toward_i - jnp.sum(weight, axis=1)[:, None, :] * imm_conc)]
    gather x24 -> x0, local copies, waits for them, and re-layouts: 22.6 us -> none  [the longest x6 10.9 us: one_block(): mob_conc[rows_here]]
  transfers between devices with their start and end apart: 6 -> 0, of which waited for: 6 -> 0; matrix products, arithmetic and copies ran while one was open for 1% -> 0% of each run, Pallas kernels for 0% -> 0%
where the time goes in v1:
time: 235 us
  Pallas kernels  230 us (98%)
  local copies, waits for them, and re-layouts  3.57 us (2%)
    pallas_call x1, Pallas kernels, on_device(): pl.pallas_call(functools.partial(exchange, n_mob, n_imm), out_shape=own +...  83.3 us
    pallas_call x1, Pallas kernels, on_device(): pl.pallas_call(functools.partial(last_reduce, n_mob, n_imm), out_shape=ow...  74.3 us
    pallas_call x2, Pallas kernels, pairs(): pl.pallas_call(functools.partial(pair_loop, step), out_shape=(jax.ShapeDt...  49.9 us
    pallas_call x1, Pallas kernels, on_device(): pl.pallas_call(functools.partial(first_gather, n_mob, n_imm), out_shape=(...  22.5 us

profile of v1, /device:TPU:0, one launch (start us, length us, event | category | flops | bytes accessed | tf_op | source)
XLA Modules:
  0.0 235.0 jit_solution(1997767456519203630)
XLA Ops:
  0.6 0.0 copy-start.5
  1.3 0.0 copy-start.4
  1.3 0.8 copy.10.mpos
  2.1 0.0 copy-done.5
  2.1 0.0 copy-start.1
  2.1 0.0 copy-done.4
  2.1 0.0 copy-start
  2.2 0.8 copy-done.1
  2.9 0.1 copy-done
  3.0 22.5 %shard_map.95 = (f32[4,2,2,16,8,128]{5,4,3,2,1,0:T(8,128)S(1)}, f32[4,2,2,16,8,128]{5,4,3,2,1,0:T(8,128)S(1)}, f32[2,16,8,128]{3,2,1,0:T(8,128)S(1)}, f32[2,16,8,128]{3,2,1,0:T(8,128)S(1)}) custom-call(f32[16,3,128]{2,1,0:T(4,128)S(1)} %copy.10.mpos, f32[2,16,3,128]{3,2,1,0:T(4,128)S(1)} %copy.11.walk, f32[16,8,128]{2,1,0:T(8,128)S(1)} %copy-done, ...), custom_call_target="tpu_custom_call" | custom-call | tf_op jit(solution)/shard_map/pallas_call | solution.py:313
  25.5 0.0 copy-start.3
  25.5 0.0 copy-start.2
  25.5 0.7 copy-done.3
  26.2 0.0 copy-done.2
  26.2 24.9 %shard_map.96 = (f32[256,8,128]{2,1,0:T(8,128)S(1)}, f32[32,8,128]{2,1,0:T(8,128)S(1)}) custom-call(s32[1,1,512]{2,1,0:T(1,128)S(1)} %copy-done.2, s32[1,1,512]{2,1,0:T(1,128)S(1)} %copy-done.3, s32[1,1]{1,0:T(1,128)S(6)} %copy.15.count, f32[256,8,128]{2,1,0:T(8,128)S(1)} %bitcast.10, f32[256,8,128]{2,1,0:T(8,128)S(1)} %bitcast.15, ...), custom_call_target="tpu_custom_call" | custom-call | tf_op jit(solution)/shard_map/pallas_call | solution.py:326
  51.1 83.3 %shard_map.97 = (f32[16,8,128]{2,1,0:T(8,128)S(1)}, f32[16,8,128]{2,1,0:T(8,128)S(1)}, f32[4,2,2,16,8,128]{5,4,3,2,1,0:T(8,128)S(1)}, f32[2,16,8,128]{3,2,1,0:T(8,128)S(1)}) custom-call(f32[4,2,2,16,8,128]{5,4,3,2,1,0:T(8,128)S(1)} %bitcast.13, f32[2,16,8,128]{3,2,1,0:T(8,128)S(1)} %bitcast.19, f32[16,8,128]{2,1,0:T(8,128)S(1)} %copy-done, ...), custom_call_target="tpu_custom_call" | custom-call | tf_op jit(solution)/shard_map/pallas_call | solution.py:354
  134.5 25.0 %shard_map.98 = (f32[256,8,128]{2,1,0:T(8,128)S(1)}, f32[32,8,128]{2,1,0:T(8,128)S(1)}) custom-call(s32[1,1,512]{2,1,0:T(1,128)S(1)} %copy-done.2, s32[1,1,512]{2,1,0:T(1,128)S(1)} %copy-done.3, s32[1,1]{1,0:T(1,128)S(6)} %copy.15.count, f32[256,8,128]{2,1,0:T(8,128)S(1)} %bitcast.11, f32[256,8,128]{2,1,0:T(8,128)S(1)} %bitcast.14, ...), custom_call_target="tpu_custom_call" | custom-call | tf_op jit(solution)/shard_map/pallas_call | solution.py:326
  159.4 74.3 %shard_map.99 = (f32[16,8,128]{2,1,0:T(8,128)S(1)}, f32[16,8,128]{2,1,0:T(8,128)S(1)}) custom-call(f32[4,2,2,16,8,128]{5,4,3,2,1,0:T(8,128)S(1)} %bitcast.12, f32[2,16,8,128]{3,2,1,0:T(8,128)S(1)} %bitcast.18, f32[16,8,128]{2,1,0:T(8,128)S(1)} %get-tuple-element.24.conc_m, f32[16,8,128]{2,1,0:T(8,128)S(1)} %get-tuple-element.25.conc_i), custom_call_target="tpu_custom_call" | custom-call | tf_op jit(solution)/shard_map/pallas_call | solution.py:363
  233.8 0.6 copy.16
  234.4 0.6 copy.17
  (2 shorter events, 0.0 us)
Async XLA Ops:
  0.6 1.4 copy-start.5
  1.3 0.8 copy-start.4
  2.1 0.8 copy-start.1
  2.1 0.8 copy-start
  25.5 0.7 copy-start.3
  25.5 0.7 copy-start.2

commit v2 on v1

--- a/solution.py
+++ b/solution.py
@@ -13,7 +13,7 @@
 CENTRE = 2.0
 MESH = pl.DeviceIdType.MESH
 VMEM_LIMIT = 48 * 1024 * 1024
-UNROLL = 4
+UNROLL = 16
 GROUPS = 6
 
 
@@ -258,8 +258,7 @@
     used = count[0, 0]
 
     def body(block, carry):
-        results = []
-        for u in range(UNROLL):
+        def weigh(u):
             k = block * UNROLL + u
             r, c = rows[0, 0, k], cols[0, 0, k]
             x = x_pos[r]
@@ -268,16 +267,31 @@
             h, m, l = split3(jnp.where(keep, x, unit))
             x_split = jnp.concatenate([h, m, l, h, m, h, zeros], axis=0).astype(jnp.bfloat16)
             power = jnp.dot(y_split[c], x_split, preferred_element_type=jnp.float32)
+            return k, r, c, power
+
+        def transfer(k, r, c, power):
             weight = jnp.exp2(power).astype(jnp.bfloat16)
             cm, ci = x_conc[r], y_conc[c]
             to_m = jnp.dot(conc_rows(ci), weight, preferred_element_type=jnp.float32)
             to_i = lax.dot_general(
                 conc_rows(cm), weight, (((1,), (1,)), ((), ())), preferred_element_type=jnp.float32
             )
+            return k, r, c, cm, ci, to_m, to_i
+
+        def finish(k, r, c, cm, ci, to_m, to_i):
             rate = jnp.where(k < used, RATE, 0.0).astype(jnp.float32)
             add_m = rate * (to_m[0:8] + to_m[8:16] - to_m[16:24] * cm)
             add_i = rate * (to_i[0:8] + to_i[8:16] - to_i[16:24] * ci)
-            results.append((r, c, add_m, add_i))
+            return r, c, add_m, add_i
+
+        weighed, moved, results = [], [], []
+        for u in range(UNROLL + 2):
+            if u < UNROLL:
+                weighed.append(weigh(u))
+            if 1 <= u <= UNROLL:
+                moved.append(transfer(*weighed[u - 1]))
+            if u >= 2:
+                results.append(finish(*moved[u - 2]))
         for r, c, add_m, add_i in results:
             gain_m[r] += add_m
             gain_i[c] += add_i

time: 235 us -> 155 us (0.66)
  Pallas kernels: 230 us -> 150 us
    pallas_call x1, Pallas kernels: 74.3 us -> 42.7 us  [on_device(): pl.pallas_call(functools.partial(last_reduce, n_mob, n_imm), out_shape=ow...]
    pallas_call x1, Pallas kernels: 83.3 us -> 53.1 us  [on_device(): pl.pallas_call(functools.partial(exchange, n_mob, n_imm), out_shape=own +...]
    pallas_call x2, Pallas kernels: 49.9 us -> 32.1 us  [pairs(): pl.pallas_call(functools.partial(pair_loop, step), out_shape=(jax.ShapeDt...]
where the time goes in v2:
time: 155 us
  Pallas kernels  150 us (97%)
  local copies, waits for them, and re-layouts  3.57 us (2%)
    pallas_call x1, Pallas kernels, on_device(): pl.pallas_call(functools.partial(exchange, n_mob, n_imm), out_shape=own +...  53.1 us
    pallas_call x1, Pallas kernels, on_device(): pl.pallas_call(functools.partial(last_reduce, n_mob, n_imm), out_shape=ow...  42.7 us
    pallas_call x2, Pallas kernels, pairs(): pl.pallas_call(functools.partial(pair_loop, step), out_shape=(jax.ShapeDt...  32.1 us
    pallas_call x1, Pallas kernels, on_device(): pl.pallas_call(functools.partial(first_gather, n_mob, n_imm), out_shape=(...  22.5 us
    unnamed x17, local copies, waits for them, and re-layouts  3.57 us

profile of v2, /device:TPU:0, one launch (start us, length us, event | category | flops | bytes accessed | tf_op | source)
XLA Modules:
  0.0 155.4 jit_solution(235010712042371106)
XLA Ops:
  0.6 0.0 copy-start.5
  1.3 0.0 copy-start.4
  1.3 0.8 copy.10.mpos
  2.1 0.0 copy-done.5
  2.1 0.0 copy-start.1
  2.1 0.0 copy-done.4
  2.1 0.0 copy-start
  2.2 0.8 copy-done.1
  2.9 0.1 copy-done
  3.0 22.5 %shard_map.95 = (f32[4,2,2,16,8,128]{5,4,3,2,1,0:T(8,128)S(1)}, f32[4,2,2,16,8,128]{5,4,3,2,1,0:T(8,128)S(1)}, f32[2,16,8,128]{3,2,1,0:T(8,128)S(1)}, f32[2,16,8,128]{3,2,1,0:T(8,128)S(1)}) custom-call(f32[16,3,128]{2,1,0:T(4,128)S(1)} %copy.10.mpos, f32[2,16,3,128]{3,2,1,0:T(4,128)S(1)} %copy.11.walk, f32[16,8,128]{2,1,0:T(8,128)S(1)} %copy-done, ...), custom_call_target="tpu_custom_call" | custom-call | tf_op jit(solution)/shard_map/pallas_call | solution.py:327
  25.5 0.0 copy-start.3
  25.5 0.0 copy-start.2
  25.5 0.7 copy-done.3
  26.2 0.0 copy-done.2
  26.2 16.0 %shard_map.96 = (f32[256,8,128]{2,1,0:T(8,128)S(1)}, f32[32,8,128]{2,1,0:T(8,128)S(1)}) custom-call(s32[1,1,512]{2,1,0:T(1,128)S(1)} %copy-done.2, s32[1,1,512]{2,1,0:T(1,128)S(1)} %copy-done.3, s32[1,1]{1,0:T(1,128)S(6)} %copy.15.count, f32[256,8,128]{2,1,0:T(8,128)S(1)} %bitcast.10, f32[256,8,128]{2,1,0:T(8,128)S(1)} %bitcast.15, ...), custom_call_target="tpu_custom_call" | custom-call | tf_op jit(solution)/shard_map/pallas_call | solution.py:340
  42.3 53.1 %shard_map.97 = (f32[16,8,128]{2,1,0:T(8,128)S(1)}, f32[16,8,128]{2,1,0:T(8,128)S(1)}, f32[4,2,2,16,8,128]{5,4,3,2,1,0:T(8,128)S(1)}, f32[2,16,8,128]{3,2,1,0:T(8,128)S(1)}) custom-call(f32[4,2,2,16,8,128]{5,4,3,2,1,0:T(8,128)S(1)} %bitcast.13, f32[2,16,8,128]{3,2,1,0:T(8,128)S(1)} %bitcast.19, f32[16,8,128]{2,1,0:T(8,128)S(1)} %copy-done, ...), custom_call_target="tpu_custom_call" | custom-call | tf_op jit(solution)/shard_map/pallas_call | solution.py:368
  95.3 16.1 %shard_map.98 = (f32[256,8,128]{2,1,0:T(8,128)S(1)}, f32[32,8,128]{2,1,0:T(8,128)S(1)}) custom-call(s32[1,1,512]{2,1,0:T(1,128)S(1)} %copy-done.2, s32[1,1,512]{2,1,0:T(1,128)S(1)} %copy-done.3, s32[1,1]{1,0:T(1,128)S(6)} %copy.15.count, f32[256,8,128]{2,1,0:T(8,128)S(1)} %bitcast.11, f32[256,8,128]{2,1,0:T(8,128)S(1)} %bitcast.14, ...), custom_call_target="tpu_custom_call" | custom-call | tf_op jit(solution)/shard_map/pallas_call | solution.py:340
  111.4 42.7 %shard_map.99 = (f32[16,8,128]{2,1,0:T(8,128)S(1)}, f32[16,8,128]{2,1,0:T(8,128)S(1)}) custom-call(f32[4,2,2,16,8,128]{5,4,3,2,1,0:T(8,128)S(1)} %bitcast.12, f32[2,16,8,128]{3,2,1,0:T(8,128)S(1)} %bitcast.18, f32[16,8,128]{2,1,0:T(8,128)S(1)} %get-tuple-element.24.conc_m, f32[16,8,128]{2,1,0:T(8,128)S(1)} %get-tuple-element.25.conc_i), custom_call_target="tpu_custom_call" | custom-call | tf_op jit(solution)/shard_map/pallas_call | solution.py:377
  154.1 0.6 copy.16
  154.7 0.6 copy.17
  (2 shorter events, 0.0 us)
Async XLA Ops:
  0.6 1.4 copy-start.5
  1.3 0.8 copy-start.4
  2.1 0.8 copy-start.1
  2.1 0.8 copy-start
  25.5 0.7 copy-start.3
  25.5 0.7 copy-start.2

commit v3 on v2

--- a/solution.py
+++ b/solution.py
@@ -13,7 +13,7 @@
 CENTRE = 2.0
 MESH = pl.DeviceIdType.MESH
 VMEM_LIMIT = 48 * 1024 * 1024
-UNROLL = 16
+UNROLL = 64
 GROUPS = 6
 
 
@@ -285,13 +285,13 @@
             return r, c, add_m, add_i
 
         weighed, moved, results = [], [], []
-        for u in range(UNROLL + 2):
+        for u in range(UNROLL + 9):
             if u < UNROLL:
                 weighed.append(weigh(u))
-            if 1 <= u <= UNROLL:
-                moved.append(transfer(*weighed[u - 1]))
-            if u >= 2:
-                results.append(finish(*moved[u - 2]))
+            if 5 <= u < UNROLL + 5:
+                moved.append(transfer(*weighed[u - 5]))
+            if u >= 9:
+                results.append(finish(*moved[u - 9]))
         for r, c, add_m, add_i in results:
             gain_m[r] += add_m
             gain_i[c] += add_i

time: 155 us -> 113 us (0.73)
  the two profiles are of different devices: /device:TPU:0 before, /device:TPU:13 now
where the time goes in v3:
time: 113 us; the launch traced here: 111 us
  Pallas kernels  106 us (94%)
  local copies, waits for them, and re-layouts  3.57 us (3%)
  between operations  1.39 us (1%)
    pallas_call x1, Pallas kernels, on_device(): pl.pallas_call(functools.partial(exchange, n_mob, n_imm), out_shape=own +...  37.8 us
    pallas_call x1, Pallas kernels, on_device(): pl.pallas_call(functools.partial(last_reduce, n_mob, n_imm), out_shape=ow...  27.7 us
    pallas_call x2, Pallas kernels, pairs(): pl.pallas_call(functools.partial(pair_loop, step), out_shape=(jax.ShapeDt...  21.1 us
    pallas_call x1, Pallas kernels, on_device(): pl.pallas_call(functools.partial(first_gather, n_mob, n_imm), out_shape=(...  20 us
    unnamed x17, local copies, waits for them, and re-layouts  3.57 us

profile of v3, /device:TPU:13, one launch (start us, length us, event | category | flops | bytes accessed | tf_op | source)
XLA Modules:
  0.0 111.4 jit_solution(8415852624384120105)
XLA Ops:
  0.6 0.0 copy-start.5
  1.3 0.0 copy-start.4
  1.3 0.8 copy.10.mpos
  2.1 0.0 copy-done.5
  2.1 0.0 copy-start.1
  2.1 0.0 copy-done.4
  2.1 0.0 copy-start
  2.2 0.8 copy-done.1
  2.9 0.1 copy-done
  3.0 20.0 %shard_map.95 = (f32[4,2,2,16,8,128]{5,4,3,2,1,0:T(8,128)S(1)}, f32[4,2,2,16,8,128]{5,4,3,2,1,0:T(8,128)S(1)}, f32[2,16,8,128]{3,2,1,0:T(8,128)S(1)}, f32[2,16,8,128]{3,2,1,0:T(8,128)S(1)}) custom-call(f32[16,3,128]{2,1,0:T(4,128)S(1)} %copy.10.mpos, f32[2,16,3,128]{3,2,1,0:T(4,128)S(1)} %copy.11.walk, f32[16,8,128]{2,1,0:T(8,128)S(1)} %copy-done, ...), custom_call_target="tpu_custom_call" | custom-call | tf_op jit(solution)/shard_map/pallas_call | solution.py:327
  23.0 0.0 copy-start.3
  23.0 0.0 copy-start.2
  23.0 0.7 copy-done.3
  23.6 0.0 copy-done.2
  23.7 10.5 %shard_map.96 = (f32[256,8,128]{2,1,0:T(8,128)S(1)}, f32[32,8,128]{2,1,0:T(8,128)S(1)}) custom-call(s32[1,1,512]{2,1,0:T(1,128)S(1)} %copy-done.2, s32[1,1,512]{2,1,0:T(1,128)S(1)} %copy-done.3, s32[1,1]{1,0:T(1,128)S(6)} %copy.15.count, f32[256,8,128]{2,1,0:T(8,128)S(1)} %bitcast.10, f32[256,8,128]{2,1,0:T(8,128)S(1)} %bitcast.15, ...), custom_call_target="tpu_custom_call" | custom-call | tf_op jit(solution)/shard_map/pallas_call | solution.py:340
  34.2 37.8 %shard_map.97 = (f32[16,8,128]{2,1,0:T(8,128)S(1)}, f32[16,8,128]{2,1,0:T(8,128)S(1)}, f32[4,2,2,16,8,128]{5,4,3,2,1,0:T(8,128)S(1)}, f32[2,16,8,128]{3,2,1,0:T(8,128)S(1)}) custom-call(f32[4,2,2,16,8,128]{5,4,3,2,1,0:T(8,128)S(1)} %bitcast.13, f32[2,16,8,128]{3,2,1,0:T(8,128)S(1)} %bitcast.19, f32[16,8,128]{2,1,0:T(8,128)S(1)} %copy-done, ...), custom_call_target="tpu_custom_call" | custom-call | tf_op jit(solution)/shard_map/pallas_call | solution.py:368
  72.0 10.5 %shard_map.98 = (f32[256,8,128]{2,1,0:T(8,128)S(1)}, f32[32,8,128]{2,1,0:T(8,128)S(1)}) custom-call(s32[1,1,512]{2,1,0:T(1,128)S(1)} %copy-done.2, s32[1,1,512]{2,1,0:T(1,128)S(1)} %copy-done.3, s32[1,1]{1,0:T(1,128)S(6)} %copy.15.count, f32[256,8,128]{2,1,0:T(8,128)S(1)} %bitcast.11, f32[256,8,128]{2,1,0:T(8,128)S(1)} %bitcast.14, ...), custom_call_target="tpu_custom_call" | custom-call | tf_op jit(solution)/shard_map/pallas_call | solution.py:340
  82.5 27.7 %shard_map.99 = (f32[16,8,128]{2,1,0:T(8,128)S(1)}, f32[16,8,128]{2,1,0:T(8,128)S(1)}) custom-call(f32[4,2,2,16,8,128]{5,4,3,2,1,0:T(8,128)S(1)} %bitcast.12, f32[2,16,8,128]{3,2,1,0:T(8,128)S(1)} %bitcast.18, f32[16,8,128]{2,1,0:T(8,128)S(1)} %get-tuple-element.24.conc_m, f32[16,8,128]{2,1,0:T(8,128)S(1)} %get-tuple-element.25.conc_i), custom_call_target="tpu_custom_call" | custom-call | tf_op jit(solution)/shard_map/pallas_call | solution.py:377
  110.2 0.6 copy.16
  110.8 0.6 copy.17
  (2 shorter events, 0.0 us)
Async XLA Ops:
  0.6 1.4 %copy-start.5 = (f32[16,3,128]{2,0,1:T(8,128)S(1)}, f32[16,3,128]{2,0,1:T(8,128)}, u32[]{:S(2)}) copy-start(f32[16,3,128]{2,0,1:T(8,128)} %param.11) | copy-start | bytes 73732
  1.3 0.8 copy-start.4
  2.1 0.8 copy-start.1
  2.1 0.8 copy-start
  23.0 0.7 copy-start.3
  23.0 0.7 copy-start.2

commit v4 on v3

--- a/solution.py
+++ b/solution.py
@@ -250,7 +250,7 @@
         y_split[c] = stacked.T.astype(jnp.bfloat16)
         return carry
 
-    lax.fori_loop(0, y_pos.shape[0], prepare, 0)
+    lax.fori_loop(0, y_pos.shape[0], prepare, 0, unroll=8)
     row = lax.broadcasted_iota(jnp.int32, (8, 128), 0)
     keep = row < 4
     unit = jnp.where(row == 4, 1.0, 0.0).astype(jnp.float32)

time: 113 us -> 107 us (0.947)
  the two profiles are of different devices: /device:TPU:13 before, /device:TPU:0 now
where the time goes in v4:
time: 107 us
  Pallas kernels  102 us (95%)
  local copies, waits for them, and re-layouts  3.57 us (3%)
  between operations  1.39 us (1%)
    pallas_call x2, Pallas kernels, pairs(): pl.pallas_call(functools.partial(pair_loop, step), out_shape=(jax.ShapeDt...  37.5 us
    pallas_call x1, Pallas kernels, on_device(): pl.pallas_call(functools.partial(exchange, n_mob, n_imm), out_shape=own +...  25.5 us
    pallas_call x1, Pallas kernels, on_device(): pl.pallas_call(functools.partial(first_gather, n_mob, n_imm), out_shape=(...  22.5 us
    pallas_call x1, Pallas kernels, on_device(): pl.pallas_call(functools.partial(last_reduce, n_mob, n_imm), out_shape=ow...  16.5 us
    unnamed x17, local copies, waits for them, and re-layouts  3.57 us

profile of v4, /device:TPU:0, one launch (start us, length us, event | category | flops | bytes accessed | tf_op | source)
XLA Modules:
  0.0 107.0 jit_solution(7115559174712265961)
XLA Ops:
  0.6 0.0 copy-start.5
  1.3 0.0 copy-start.4
  1.3 0.8 copy.10.mpos
  2.1 0.0 copy-done.5
  2.1 0.0 copy-start.1
  2.1 0.0 copy-done.4
  2.1 0.0 copy-start
  2.2 0.8 copy-done.1
  2.9 0.1 copy-done
  3.0 22.5 %shard_map.95 = (f32[4,2,2,16,8,128]{5,4,3,2,1,0:T(8,128)S(1)}, f32[4,2,2,16,8,128]{5,4,3,2,1,0:T(8,128)S(1)}, f32[2,16,8,128]{3,2,1,0:T(8,128)S(1)}, f32[2,16,8,128]{3,2,1,0:T(8,128)S(1)}) custom-call(f32[16,3,128]{2,1,0:T(4,128)S(1)} %copy.10.mpos, f32[2,16,3,128]{3,2,1,0:T(4,128)S(1)} %copy.11.walk, f32[16,8,128]{2,1,0:T(8,128)S(1)} %copy-done, ...), custom_call_target="tpu_custom_call" | custom-call | tf_op jit(solution)/shard_map/pallas_call | solution.py:327
  25.5 0.0 copy-start.3
  25.5 0.0 copy-start.2
  25.5 0.7 copy-done.3
  26.2 0.0 copy-done.2
  26.2 18.7 %shard_map.96 = (f32[256,8,128]{2,1,0:T(8,128)S(1)}, f32[32,8,128]{2,1,0:T(8,128)S(1)}) custom-call(s32[1,1,512]{2,1,0:T(1,128)S(1)} %copy-done.2, s32[1,1,512]{2,1,0:T(1,128)S(1)} %copy-done.3, s32[1,1]{1,0:T(1,128)S(6)} %copy.15.count, f32[256,8,128]{2,1,0:T(8,128)S(1)} %bitcast.10, f32[256,8,128]{2,1,0:T(8,128)S(1)} %bitcast.15, ...), custom_call_target="tpu_custom_call" | custom-call | tf_op jit(solution)/shard_map/pallas_call | solution.py:340
  44.9 25.5 %shard_map.97 = (f32[16,8,128]{2,1,0:T(8,128)S(1)}, f32[16,8,128]{2,1,0:T(8,128)S(1)}, f32[4,2,2,16,8,128]{5,4,3,2,1,0:T(8,128)S(1)}, f32[2,16,8,128]{3,2,1,0:T(8,128)S(1)}) custom-call(f32[4,2,2,16,8,128]{5,4,3,2,1,0:T(8,128)S(1)} %bitcast.13, f32[2,16,8,128]{3,2,1,0:T(8,128)S(1)} %bitcast.19, f32[16,8,128]{2,1,0:T(8,128)S(1)} %copy-done, ...), custom_call_target="tpu_custom_call" | custom-call | tf_op jit(solution)/shard_map/pallas_call | solution.py:368
  70.4 18.7 %shard_map.98 = (f32[256,8,128]{2,1,0:T(8,128)S(1)}, f32[32,8,128]{2,1,0:T(8,128)S(1)}) custom-call(s32[1,1,512]{2,1,0:T(1,128)S(1)} %copy-done.2, s32[1,1,512]{2,1,0:T(1,128)S(1)} %copy-done.3, s32[1,1]{1,0:T(1,128)S(6)} %copy.15.count, f32[256,8,128]{2,1,0:T(8,128)S(1)} %bitcast.11, f32[256,8,128]{2,1,0:T(8,128)S(1)} %bitcast.14, ...), custom_call_target="tpu_custom_call" | custom-call | tf_op jit(solution)/shard_map/pallas_call | solution.py:340
  89.2 16.5 %shard_map.99 = (f32[16,8,128]{2,1,0:T(8,128)S(1)}, f32[16,8,128]{2,1,0:T(8,128)S(1)}) custom-call(f32[4,2,2,16,8,128]{5,4,3,2,1,0:T(8,128)S(1)} %bitcast.12, f32[2,16,8,128]{3,2,1,0:T(8,128)S(1)} %bitcast.18, f32[16,8,128]{2,1,0:T(8,128)S(1)} %get-tuple-element.24.conc_m, f32[16,8,128]{2,1,0:T(8,128)S(1)} %get-tuple-element.25.conc_i), custom_call_target="tpu_custom_call" | custom-call | tf_op jit(solution)/shard_map/pallas_call | solution.py:377
  105.7 0.6 copy.16
  106.3 0.6 copy.17
  (2 shorter events, 0.0 us)
Async XLA Ops:
  0.6 1.4 %copy-start.5 = (f32[16,3,128]{2,0,1:T(8,128)S(1)}, f32[16,3,128]{2,0,1:T(8,128)}, u32[]{:S(2)}) copy-start(f32[16,3,128]{2,0,1:T(8,128)} %param.11) | copy-start | bytes 73732
  1.3 0.8 copy-start.4
  2.1 0.8 copy-start.1
  2.1 0.8 copy-start
  25.5 0.7 copy-start.3
  25.5 0.7 copy-start.2
